TPU v7x, 32 devices: a whole 2x2x4 slice. The times are simulated.
32 devices in a mesh: fsdp: 8 (over y, x, core), tp: 4 (over z).
Axes of the slice: x: 2, y: 2, z: 4, core: 2. Of those that a mesh axis runs over, the one named last changes fastest.
Arguments:
- hidden_in: bfloat16 [4096, 2048], P(('fsdp', 'tp')), may hold values from -6 to 6
- cotangent: bfloat16 [4096, 2048], P(('fsdp', 'tp')), may hold values from -6 to 6
- segment_ids: int32 [8, 512], P('fsdp'), may hold values from 0 to 3, never falling along the last dimension, each value on 1 to 256 neighbouring positions
- adapter_set: int32 [8], P('fsdp'), may hold values from 0 to 7
- qkv_weight: bfloat16 [3, 2048, 2048], P(None, 'fsdp', 'tp'), may hold values from -0.125 to 0.125
- qkv_bias: bfloat16 [2, 2048], P(None, 'tp'), may hold values from -3 to 3
- proj_weight: bfloat16 [2048, 2048], P('tp', 'fsdp'), may hold values from -1.5 to 1.5
- proj_bias: bfloat16 [2048], replicated, may hold values from -3 to 3
- up_weight: bfloat16 [2048, 8192], P('fsdp', 'tp'), may hold values from -0.125 to 0.125
- up_bias: bfloat16 [8192], P('tp'), may hold values from -3 to 3
- down_weight: bfloat16 [8192, 2048], P('tp', 'fsdp'), may hold values from -0.0625 to 0.0625
- down_bias: bfloat16 [2048], replicated, may hold values from -3 to 3
- norm_gain: bfloat16 [2, 2048], replicated, may hold values from 0.5 to 1.5
- norm_bias: bfloat16 [2, 2048], replicated, may hold values from -3 to 3
- qkv_adapt_in: bfloat16 [3, 8, 2048, 16], replicated, may hold values from -0.125 to 0.125
- qkv_adapt_out: bfloat16 [3, 8, 16, 2048], P(None, None, None, 'tp'), may hold values from -0.75 to 0.75
- attn_adapt_in: bfloat16 [8, 2048, 16], P(None, 'tp'), may hold values from -1.5 to 1.5
- attn_adapt_out: bfloat16 [8, 16, 2048], replicated, may hold values from -0.75 to 0.75
- up_adapt_in: bfloat16 [8, 2048, 16], replicated, may hold values from -0.125 to 0.125
- up_adapt_out: bfloat16 [8, 16, 8192], P(None, None, 'tp'), may hold values from -0.75 to 0.75
- down_adapt_in: bfloat16 [8, 8192, 16], P(None, 'tp'), may hold values from -0.0625 to 0.0625
- down_adapt_out: bfloat16 [8, 16, 2048], replicated, may hold values from -0.75 to 0.75
Outputs:
- layer_out: float32 [4096, 2048], P(('fsdp', 'tp'))
- grad_input: float32 [4096, 2048], P(('fsdp', 'tp'))
- grad_qkv_in: float32 [3, 8, 2048, 16], replicated
- grad_qkv_out: float32 [3, 8, 16, 2048], P(None, None, None, 'tp')
- grad_attn_in: float32 [8, 2048, 16], P(None, 'tp')
- grad_attn_out: float32 [8, 16, 2048], replicated
- grad_up_in: float32 [8, 2048, 16], replicated
- grad_up_out: float32 [8, 16, 8192], P(None, None, 'tp')
- grad_down_in: float32 [8, 8192, 16], P(None, 'tp')
- grad_down_out: float32 [8, 16, 2048], replicated
Inputs may be any that keep to these rules, and one draw needn't show every extreme that they name: `segment_ids`: within a sequence the numbers never fall; each of the 4 documents holds 1 to 256 tokens and one holds exactly 256.
All inputs are finite; a program needn't handle non-finite values.
Results may differ from a plain program's by a relative error of at most 0.018.
Values may be sent and summed in bfloat16 or wider, within the bound.
A program may use at most 192 MiB of HBM per device.

v0:
```python
import functools
import math

import jax
import jax.numpy as jnp
from jax import lax
from jax.experimental import pallas as pl
from jax.experimental.pallas import tpu as pltpu
from jax.sharding import PartitionSpec as P

HEAD = 128
RANK = 16
MESH = pl.DeviceIdType.MESH
F32 = jnp.float32
BF16 = jnp.bfloat16
ROOT = math.sqrt(2.0 / math.pi)


def layer_norm(field_in, gain_row, shift_row):
    centre = jnp.mean(field_in, axis=-1, keepdims=True)
    centred = field_in - centre
    spread = jnp.mean(centred * centred, axis=-1, keepdims=True)
    return centred * lax.rsqrt(spread + 1e-05) * gain_row + shift_row


def precise_dot(left, right):
    return jnp.dot(left, right, precision=lax.Precision.HIGHEST)


def mixed_dot(left, right):
    return jnp.dot(left, right, preferred_element_type=jnp.float32)


def choose_set(table, index, axis):
    return lax.dynamic_index_in_dim(table, index, axis, keepdims=False)


def place_set(grad, index, sets, axis):
    onehot = (jnp.arange(sets) == index).astype(jnp.float32)
    shape_list = [1] * (grad.ndim + 1)
    shape_list[axis] = sets
    return jnp.expand_dims(grad, axis) * onehot.reshape(shape_list)


def per_device(
    hidden_in,
    cotangent,
    segment_ids,
    adapter_set,
    qkv_weight,
    qkv_bias,
    proj_weight,
    proj_bias,
    up_weight,
    up_bias,
    down_weight,
    down_bias,
    norm_gain,
    norm_bias,
    qkv_adapt_in,
    qkv_adapt_out,
    attn_adapt_in,
    attn_adapt_out,
    up_adapt_in,
    up_adapt_out,
    down_adapt_in,
    down_adapt_out,
):
    width_local = qkv_weight.shape[2]
    heads_local = width_local // HEAD
    sets = qkv_adapt_in.shape[1]
    chosen = adapter_set[0]
    segments = segment_ids[0]
    seq_rows = segments.shape[0]
    block_rows = min(512, seq_rows)
    blocks = seq_rows // block_rows
    score_scale = 1.0 / math.sqrt(HEAD)
    gains = norm_gain.astype(jnp.float32)
    shifts = norm_bias.astype(jnp.float32)
    first_q = choose_set(qkv_adapt_in, chosen, 1)
    second_q = choose_set(qkv_adapt_out, chosen, 1)
    first_o = choose_set(attn_adapt_in, chosen, 0)
    second_o = choose_set(attn_adapt_out, chosen, 0)
    first_u = choose_set(up_adapt_in, chosen, 0)
    second_u = choose_set(up_adapt_out, chosen, 0)
    first_d = choose_set(down_adapt_in, chosen, 0)
    second_d = choose_set(down_adapt_out, chosen, 0)
    seq_hidden = lax.all_gather(hidden_in, "tp", axis=0, tiled=True)
    qkv_full, proj_full = (
        lax.all_gather(qkv_weight, "fsdp", axis=1, tiled=True),
        lax.all_gather(proj_weight, "fsdp", axis=1, tiled=True),
    )
    main_term = jnp.einsum("sd,jdc->jsc", seq_hidden, qkv_full, preferred_element_type=jnp.float32)
    low_in = jnp.einsum("sd,jdr->jsr", seq_hidden, first_q, preferred_element_type=jnp.float32)
    low_term = jnp.einsum(
        "jsr,jrc->jsc", low_in, second_q.astype(jnp.float32), precision=lax.Precision.HIGHEST
    )
    bias_rows = jnp.stack([qkv_bias[0], jnp.zeros_like(qkv_bias[0]), qkv_bias[1]]).astype(
        jnp.float32
    )[:, None, :]
    qkv_round = (main_term + low_term + bias_rows).astype(jnp.bfloat16)
    queries = qkv_round[0].reshape(seq_rows, heads_local, HEAD)
    keys = qkv_round[1].reshape(seq_rows, heads_local, HEAD)
    values = qkv_round[2].reshape(seq_rows, heads_local, HEAD)
    query_blocks = queries.reshape(blocks, block_rows, heads_local, HEAD)
    seg_blocks = segments.reshape(blocks, block_rows)

    def scores_of(query_rows, seg_rows):
        raw_scores = (
            jnp.einsum("bhe,she->hbs", query_rows, keys, preferred_element_type=jnp.float32)
            * score_scale
        )
        same_doc = (seg_rows[:, None] == segments[None, :])[None]
        return jnp.where(same_doc, raw_scores, -1e30)

    def forward_block(inputs):
        query_rows, seg_rows = inputs
        scores = scores_of(query_rows, seg_rows)
        row_top = jnp.max(scores, axis=-1, keepdims=True)
        weights = jnp.exp(scores - row_top)
        row_total = jnp.sum(weights, axis=-1, keepdims=True)
        attn_probs = (weights / row_total).astype(jnp.bfloat16)
        attn_mixed = jnp.einsum(
            "hbs,she->bhe", attn_probs, values, preferred_element_type=jnp.float32
        )
        return (attn_mixed, (row_top + jnp.log(row_total))[..., 0])

    attn_mixed, logsum = lax.map(forward_block, (query_blocks, seg_blocks))
    attended = attn_mixed.reshape(seq_rows, width_local).astype(jnp.bfloat16)
    low_attn = mixed_dot(attended, first_o)
    second_o_wide = second_o.astype(jnp.float32)
    row_part = attended
    low_part = low_attn
    attn_sum = lax.psum_scatter(
        mixed_dot(row_part, proj_full) + precise_dot(low_part, second_o_wide),
        "tp",
        scatter_dimension=0,
        tiled=True,
    )
    first_sum = hidden_in.astype(jnp.float32) + attn_sum + proj_bias.astype(jnp.float32)
    normed = layer_norm(first_sum, gains[0], shifts[0])
    normed_round = normed.astype(jnp.bfloat16)
    seq_normed = lax.all_gather(normed_round, "tp", axis=0, tiled=True)
    up_full, down_full = (
        lax.all_gather(up_weight, "fsdp", axis=0, tiled=True),
        lax.all_gather(down_weight, "fsdp", axis=1, tiled=True),
    )
    low_up = mixed_dot(seq_normed, first_u)
    pre_act = (
        mixed_dot(seq_normed, up_full)
        + precise_dot(low_up, second_u.astype(jnp.float32))
        + up_bias.astype(jnp.float32)
    )
    act_round = jax.nn.gelu(pre_act, approximate=True).astype(jnp.bfloat16)
    low_down = mixed_dot(act_round, first_d)
    second_d_wide = second_d.astype(jnp.float32)
    row_part = act_round
    low_part = low_down
    ffn_sum = lax.psum_scatter(
        mixed_dot(row_part, down_full) + precise_dot(low_part, second_d_wide),
        "tp",
        scatter_dimension=0,
        tiled=True,
    )
    second_sum = normed + ffn_sum + down_bias.astype(jnp.float32)
    layer_out = layer_norm(second_sum, gains[1], shifts[1])
    unused, norm_back = jax.vjp(
        lambda field_in: layer_norm(field_in, gains[1], shifts[1]), second_sum
    )
    grad_second = norm_back(cotangent.astype(jnp.float32))[0]
    grad_feed_round = grad_second.astype(jnp.bfloat16)
    seq_grad_feed = lax.all_gather(grad_feed_round, "tp", axis=0, tiled=True)
    up_back, down_back = (
        lax.all_gather(up_weight, "fsdp", axis=0, tiled=True),
        lax.all_gather(down_weight, "fsdp", axis=1, tiled=True),
    )
    grad_low_down = mixed_dot(seq_grad_feed, second_d.T)
    grad_act = jnp.einsum(
        "sd,fd->sf", seq_grad_feed, down_back, preferred_element_type=jnp.float32
    ) + precise_dot(grad_low_down, first_d.astype(jnp.float32).T)
    unused, gelu_back = jax.vjp(lambda field_in: jax.nn.gelu(field_in, approximate=True), pre_act)
    grad_pre_round = gelu_back(grad_act)[0].astype(jnp.bfloat16)
    grad_down_out_part = precise_dot(low_down.T, seq_grad_feed.astype(jnp.float32))
    grad_down_in_part = precise_dot(act_round.astype(jnp.float32).T, grad_low_down)
    grad_low_up = mixed_dot(grad_pre_round, second_u.T)
    grad_up_out_part = precise_dot(low_up.T, grad_pre_round.astype(jnp.float32))
    grad_up_in_part = precise_dot(seq_normed.astype(jnp.float32).T, grad_low_up)
    first_u_wide = first_u.astype(jnp.float32)
    row_part = grad_pre_round
    low_part = grad_low_up
    grad_normed = grad_second + lax.psum_scatter(
        jnp.einsum("sf,df->sd", row_part, up_back, preferred_element_type=jnp.float32)
        + precise_dot(low_part, first_u_wide.T),
        "tp",
        scatter_dimension=0,
        tiled=True,
    )
    unused, norm_front = jax.vjp(
        lambda field_in: layer_norm(field_in, gains[0], shifts[0]), first_sum
    )
    grad_first = norm_front(grad_normed)[0]
    grad_branch_round = grad_first.astype(jnp.bfloat16)
    seq_grad_branch = lax.all_gather(grad_branch_round, "tp", axis=0, tiled=True)
    qkv_back, proj_back = (
        lax.all_gather(qkv_weight, "fsdp", axis=1, tiled=True),
        lax.all_gather(proj_weight, "fsdp", axis=1, tiled=True),
    )
    grad_low_attn = mixed_dot(seq_grad_branch, second_o.T)
    grad_attended = jnp.einsum(
        "sd,cd->sc", seq_grad_branch, proj_back, preferred_element_type=jnp.float32
    ) + precise_dot(grad_low_attn, first_o.astype(jnp.float32).T)
    grad_attended_round = grad_attended.astype(jnp.bfloat16)
    grad_attn_out_part = precise_dot(low_attn.T, seq_grad_branch.astype(jnp.float32))
    grad_attn_in_part = precise_dot(attended.astype(jnp.float32).T, grad_low_attn)
    grad_blocks = grad_attended_round.reshape(blocks, block_rows, heads_local, HEAD)

    def backward_block(carry, inputs):
        grad_keys, grad_values = carry
        query_rows, seg_rows, lse_rows, grad_rows = inputs
        scores = scores_of(query_rows, seg_rows)
        attn_probs = jnp.exp(scores - lse_rows[..., None])
        grad_probs = jnp.einsum(
            "bhe,she->hbs", grad_rows, values, preferred_element_type=jnp.float32
        )
        centre = jnp.sum(grad_probs * attn_probs, axis=-1, keepdims=True)
        grad_scores = (attn_probs * (grad_probs - centre)).astype(jnp.bfloat16)
        grad_query = (
            jnp.einsum("hbs,she->bhe", grad_scores, keys, preferred_element_type=jnp.float32)
            * score_scale
        )
        grad_keys = (
            grad_keys
            + jnp.einsum(
                "hbs,bhe->she", grad_scores, query_rows, preferred_element_type=jnp.float32
            )
            * score_scale
        )
        grad_values = grad_values + jnp.einsum(
            "hbs,bhe->she",
            attn_probs.astype(jnp.bfloat16),
            grad_rows,
            preferred_element_type=jnp.float32,
        )
        return ((grad_keys, grad_values), grad_query)

    zero_state = jnp.zeros((seq_rows, heads_local, HEAD), jnp.float32)
    key_value_grads, grad_queries = lax.scan(
        backward_block, (zero_state, zero_state), (query_blocks, seg_blocks, logsum, grad_blocks)
    )
    grad_qkv_round = jnp.stack(
        [
            grad_queries.reshape(seq_rows, width_local),
            key_value_grads[0].reshape(seq_rows, width_local),
            key_value_grads[1].reshape(seq_rows, width_local),
        ]
    ).astype(jnp.bfloat16)
    grad_qkv_out_part = jnp.einsum(
        "jsr,jsc->jrc", low_in, grad_qkv_round.astype(jnp.float32), precision=lax.Precision.HIGHEST
    )
    grad_low_qkv = jnp.einsum(
        "jsc,jrc->jsr", grad_qkv_round, second_q, preferred_element_type=jnp.float32
    )
    grad_qkv_in_part = jnp.einsum(
        "sd,jsr->jdr", seq_hidden.astype(jnp.float32), grad_low_qkv, precision=lax.Precision.HIGHEST
    )
    first_q_wide = first_q.astype(jnp.float32)
    row_part = grad_qkv_round
    low_part = grad_low_qkv
    grad_input = grad_first + lax.psum_scatter(
        (
            jnp.einsum("jsc,jdc->sd", row_part, qkv_back, preferred_element_type=jnp.float32)
            + jnp.einsum("jsr,jdr->sd", low_part, first_q_wide, precision=lax.Precision.HIGHEST)
        ).astype(jnp.bfloat16),
        "tp",
        scatter_dimension=0,
        tiled=True,
    ).astype(jnp.float32)
    wide_grads = lax.psum(
        (
            place_set(grad_qkv_in_part, chosen, sets, 1),
            place_set(grad_attn_out_part, chosen, sets, 0),
            place_set(grad_up_in_part, chosen, sets, 0),
            place_set(grad_down_out_part, chosen, sets, 0),
        ),
        ("fsdp", "tp"),
    )
    split_grads = (
        lax.psum(place_set(grad_qkv_out_part, chosen, sets, 1).astype(jnp.bfloat16), "fsdp").astype(
            jnp.float32
        ),
        lax.psum(place_set(grad_attn_in_part, chosen, sets, 0).astype(jnp.bfloat16), "fsdp").astype(
            jnp.float32
        ),
        lax.psum(place_set(grad_up_out_part, chosen, sets, 0).astype(jnp.bfloat16), "fsdp").astype(
            jnp.float32
        ),
        lax.psum(place_set(grad_down_in_part, chosen, sets, 0).astype(jnp.bfloat16), "fsdp").astype(
            jnp.float32
        ),
    )
    return (
        layer_out,
        grad_input,
        wide_grads[0],
        split_grads[0],
        split_grads[1],
        wide_grads[1],
        wide_grads[2],
        split_grads[2],
        split_grads[3],
        wide_grads[3],
    )


def dot_nn(left, right):
    return jnp.dot(left, right, preferred_element_type=F32)


def dot_nt(left, right):
    return lax.dot_general(left, right, (((1,), (1,)), ((), ())), preferred_element_type=F32)


def flip(index, mask):
    out, bit = index, 1
    while bit <= mask:
        if mask & bit:
            out = out + bit - 2 * bit * lax.rem(lax.div(index, bit), 2)
        bit *= 2
    return out


def norm_parts(rows):
    centred = rows - jnp.mean(rows, axis=-1, keepdims=True)
    spread = jnp.mean(centred * centred, axis=-1, keepdims=True)
    rstd = lax.rsqrt(spread + 1e-05)
    return centred * rstd, rstd


def norm_pull(grad, unit, rstd):
    return rstd * (
        grad
        - jnp.mean(grad, axis=-1, keepdims=True)
        - unit * jnp.mean(grad * unit, axis=-1, keepdims=True)
    )


class Gather:
    def __init__(self, which, shard, whole, send, recv, fsdp, tp, count):
        self.which, self.shard, self.whole = which, shard, whole
        self.send, self.recv, self.fsdp, self.tp = send, recv, fsdp, tp
        bits = [1 << i for i in range(1, count.bit_length() - 1)]
        self.orders = [bits, bits[::-1]]
        self.steps = len(bits)
        self.held = [[0], [0]]
        self.sent = []
        self.count = count

    def copy(self, half, mask, bit):
        landed = mask ^ bit
        place = self.whole(flip(self.fsdp, mask), half)
        return pltpu.make_async_remote_copy(
            src_ref=self.shard(half) if mask == 0 else place,
            dst_ref=place,
            send_sem=self.send.at[self.which, half, landed],
            recv_sem=self.recv.at[self.which, half, landed],
            device_id=(flip(self.fsdp, bit), self.tp),
            device_id_type=MESH,
        )

    def launch(self, half, mask, bit):
        self.copy(half, mask, bit).start()
        self.sent.append((half, mask, bit))

    def await_block(self, half, mask, bit):
        place = self.whole(flip(self.fsdp, mask), half)
        pltpu.make_async_remote_copy(
            src_ref=place,
            dst_ref=place,
            send_sem=self.send.at[self.which, half, mask],
            recv_sem=self.recv.at[self.which, half, mask],
            device_id=(flip(self.fsdp, bit), self.tp),
            device_id_type=MESH,
        ).wait_recv()

    def stage(self, step):
        for half in range(2):
            fresh = [0]
            if step > 0:
                bit = self.orders[half][step - 1]
                fresh = [mask ^ bit for mask in self.held[half]]
                for mask in fresh:
                    self.await_block(half, mask, bit)
                self.held[half] = self.held[half] + fresh
            if step < self.steps:
                for mask in self.held[half]:
                    self.launch(half, mask, self.orders[half][step])
            for mask in fresh:
                self.launch(half, mask, 1)

    def finish(self):
        for half in range(2):
            for mask in self.held[half]:
                self.await_block(half, mask ^ 1, 1)

    def drain(self):
        for half, mask, bit in self.sent:
            self.copy(half, mask, bit).wait_send()


def layer_kernel(cfg, *refs):
    F, T, S, D, H, FL, C = (cfg[k] for k in ("F", "T", "S", "D", "H", "FL", "C"))
    Q, heads, block = S // T, H // HEAD, D // F
    R = Q // C
    M = T * R
    NT = math.gcd(FL, 512)
    (
        hidden_in, cotangent, segments, chosen, qkv_w, proj_w, up_w, down_w,
        proj_bias, down_bias, up_bias, qkv_bias, gains, shifts,
        q_in, q_out, o_in, o_out, u_in, u_out, d_in, d_out,
        layer_out, grad_input, feed_all, units_all, mix_all, heads_all,
        hidden, qkv_all, proj_all, up_all, down_all,
        qkv, probs, mixed, normed, act, slope, grad_feed, grad_branch, grad_mixed, grad_qkv,
        part, from_low, from_high, unit_one, rstd_one, grad_own,
        low_q, low_o, low_u, low_d, back_q, back_o, back_u, back_d,
        seg_row, seg_col, turned,
        wide_f, heads_f, units_f, wide_stage, heads_stage, units_stage,
        feed_part, feed_land, feed_full, mix_part, mix_land, mix_full, units_g, heads_g,
        stage_sem, deal_send, deal_recv,
        w_send, w_recv, up_send, up_recv, dn_send, dn_recv, g_up_send, g_up_recv, g_dn_send, g_dn_recv,
        own_sem,
    ) = refs
    grad_pre = slope
    f, z = lax.axis_index("fsdp"), lax.axis_index("tp")
    bits = [1 << i for i in range(F.bit_length() - 1)]

    barrier = pltpu.get_barrier_semaphore()
    for bit in bits:
        pl.semaphore_signal(barrier, inc=1, device_id=(flip(f, bit), z), device_id_type=MESH)

    turns = [lax.rem(z + k, T) for k in range(T)]
    for k in range(1, T):
        pl.semaphore_signal(barrier, inc=1, device_id=(f, turns[k]), device_id_type=MESH)
    pl.semaphore_wait(barrier, len(bits) + T - 1)

    rows_of = lambda total, half: pl.ds(half * (total // 2), total // 2)
    gathers = [
        Gather(0, lambda h: qkv_w.at[:, rows_of(block, h)], lambda g, h: qkv_all.at[:, g, rows_of(block, h)], w_send, w_recv, f, z, F),
        Gather(1, lambda h: proj_w.at[rows_of(H, h)], lambda g, h: proj_all.at[g, rows_of(H, h)], w_send, w_recv, f, z, F),
        Gather(2, lambda h: up_w.at[rows_of(block, h)], lambda g, h: up_all.at[g, rows_of(block, h)], w_send, w_recv, f, z, F),
    ]
    quarter = lambda part, h: pl.ds((2 * part + h) * (FL // 4), FL // 4)
    for part_of in range(2):
        shard = lambda h, p=part_of: down_w.at[quarter(p, h)]
        whole = lambda g, h, p=part_of: down_all.at[g, quarter(p, h)]
        gathers.append(Gather(3 + part_of, shard, whole, w_send, w_recv, f, z, F))
    pair = lambda ref, n: lambda h: ref.at[..., rows_of(n, h), :]
    pair_all = lambda ref, n: lambda g, h: ref.at[g, ..., rows_of(n, h), :]
    for k, (shard, whole) in enumerate(
        [(feed_full, feed_all), (units_g, units_all), (mix_full, mix_all), (heads_g, heads_all)]
    ):
        n = shard.shape[-2]
        gathers.append(Gather(5 + k, pair(shard, n), pair_all(whole, n), w_send, w_recv, f, z, F))
    K = gathers[0].steps
    own_copies = [
        pltpu.make_async_copy(hidden_in, hidden.at[:, z], own_sem.at[0]),
        pltpu.make_async_copy(qkv_w, qkv_all.at[:, f], own_sem.at[1]),
        pltpu.make_async_copy(proj_w, proj_all.at[f], own_sem.at[2]),
        pltpu.make_async_copy(up_w, up_all.at[f], own_sem.at[3]),
        pltpu.make_async_copy(down_w, down_all.at[f], own_sem.at[4]),
    ]
    own_grads = [
        pltpu.make_async_copy(feed_full, feed_all.at[f], own_sem.at[5]),
        pltpu.make_async_copy(units_g, units_all.at[f], own_sem.at[6]),
        pltpu.make_async_copy(mix_full, mix_all.at[f], own_sem.at[7]),
        pltpu.make_async_copy(heads_g, heads_all.at[f], own_sem.at[8]),
    ]

    def deal_copy(which, k):
        part_ref, land_ref = exchanges[which]
        return pltpu.make_async_remote_copy(
            src_ref=part_ref, dst_ref=land_ref.at[k - 1],
            send_sem=deal_send.at[which, k - 1], recv_sem=deal_recv.at[which, k - 1],
            device_id=(f, turns[k]), device_id_type=MESH,
        )

    exchanges = [(feed_part, feed_land), (mix_part, mix_land)]

    def deal(which):
        for k in range(1, T):
            deal_copy(which, k).start()

    def collect(which):
        part_ref, land_ref = exchanges[which]
        total = part_ref[...].astype(F32)
        for k in range(1, T):
            deal_copy(which, k).wait_recv()
            total += land_ref[k - 1].astype(F32)
        return total.astype(BF16)

    def pass_on(which):
        for k in (2 * which, 2 * which + 1):
            own_grads[k].start()
            gathers[5 + k].stage(0)

    def pass_drain(which):
        for k in range(1, T):
            deal_copy(which, k).wait_send()
        for k in (2 * which, 2 * which + 1):
            own_grads[k].wait()

    def line_copy(src, dst, send, recv, c, q, step):
        return pltpu.make_async_remote_copy(
            src_ref=src, dst_ref=dst, send_sem=send.at[c, q], recv_sem=recv.at[c, q],
            device_id=(f, z + step), device_id_type=MESH,
        )

    def rs_copy(c, q, step):
        landing, send, recv = (from_low, up_send, up_recv) if step > 0 else (from_high, dn_send, dn_recv)
        return line_copy(part.at[c, q], landing.at[c, q], send, recv, c, q, step)

    def rs_wait(c, q, step):
        landing, send, recv = (from_low, up_send, up_recv) if step > 0 else (from_high, dn_send, dn_recv)
        line_copy(landing.at[c, q], landing.at[c, q], send, recv, c, q, -step).wait_recv()

    def rs(c, t):
        def add(q, landing):
            part[c, q] = part[c, q] + landing[c, q]

        @pl.when(z <= t - 1)
        def _():
            q = T - t + z

            @pl.when(z > 0)
            def _():
                rs_wait(c, q, 1)
                add(q, from_low)

            rs_copy(c, q, 1).start()

        @pl.when(z >= T - t)
        def _():
            q = z - (T - t)

            @pl.when(z < T - 1)
            def _():
                rs_wait(c, q, -1)
                add(q, from_high)

            rs_copy(c, q, -1).start()

    def rs_end(c):
        @pl.when(z > 0)
        def _():
            rs_wait(c, z, 1)

        @pl.when(z < T - 1)
        def _():
            rs_wait(c, z, -1)

    def rs_sum(c, rows):
        terms = [ref[c, z, rows].astype(F32) for ref in (part, from_low, from_high)]
        return (terms[0] + terms[1]) + terms[2]

    def rs_drain(c):
        for q in range(T):
            if q > 0:

                @pl.when(z < q)
                def _(q=q):
                    rs_copy(c, q, 1).wait_send()

            if q < T - 1:

                @pl.when(z > q)
                def _(q=q):
                    rs_copy(c, q, -1).wait_send()

    def ag_copy(buffer, c, q, step):
        send, recv = (g_up_send, g_up_recv) if step > 0 else (g_dn_send, g_dn_recv)
        if c is None:
            return line_copy(buffer.at[:, q], buffer.at[:, q], send, recv, C, q, step)
        return line_copy(buffer.at[c, q], buffer.at[c, q], send, recv, c, q, step)

    def ag_wait(buffer, c, q, step):
        send, recv = (g_up_send, g_up_recv) if step > 0 else (g_dn_send, g_dn_recv)
        place = buffer.at[:, q] if c is None else buffer.at[c, q]
        line_copy(place, place, send, recv, C if c is None else c, q, -step).wait_recv()

    def ag(buffer, c, t):
        if t == 1:

            @pl.when(z < T - 1)
            def _():
                ag_copy(buffer, c, z, 1).start()

            @pl.when(z > 0)
            def _():
                ag_copy(buffer, c, z, -1).start()

            return

        @pl.when(z >= t - 1)
        def _():
            q = z - (t - 1)
            ag_wait(buffer, c, q, 1)

            @pl.when(z < T - 1)
            def _():
                ag_copy(buffer, c, q, 1).start()

        @pl.when(z <= T - t)
        def _():
            q = z + (t - 1)
            ag_wait(buffer, c, q, -1)

            @pl.when(z > 0)
            def _():
                ag_copy(buffer, c, q, -1).start()

    def ag_drain(buffer, c):
        for q in range(T):

            @pl.when((z >= q) & (z < T - 1))
            def _(q=q):
                ag_copy(buffer, c, q, 1).wait_send()

            @pl.when((z <= q) & (z > 0))
            def _(q=q):
                ag_copy(buffer, c, q, -1).wait_send()

    a_q = lambda j: wide_f.at[j]
    b_o, a_u, b_d = wide_f.at[3], wide_f.at[4], wide_f.at[5]
    b_q = lambda j: heads_f.at[j]
    a_o = heads_f.at[3]
    b_u, a_d = units_f.at[0], units_f.at[1]
    line = lambda ref, k: ref[pl.ds(k, 1)].astype(F32)
    flat = lambda ref: ref[...].reshape(1, ref.shape[0]).astype(F32)
    sets = q_in.shape[1]
    pick = (lax.broadcasted_iota(jnp.int32, (sets, 128), 0) == chosen[...]).astype(F32)

    def stage_copies(s):
        slot = s % 2
        pairs = [
            (q_in.at[:, s], wide_stage.at[slot, pl.ds(0, 3)]),
            (o_out.at[s], wide_stage.at[slot, 3]),
            (u_in.at[s], wide_stage.at[slot, 4]),
            (d_out.at[s], wide_stage.at[slot, 5]),
            (q_out.at[:, s], heads_stage.at[slot, pl.ds(0, 3)]),
            (o_in.at[s], heads_stage.at[slot, 3]),
            (u_out.at[s], units_stage.at[slot, 0]),
            (d_in.at[s], units_stage.at[slot, 1]),
        ]
        return [
            pltpu.make_async_copy(src, dst, stage_sem.at[slot, k])
            for k, (src, dst) in enumerate(pairs)
        ]

    def choose(s):
        for copy in stage_copies(s):
            copy.wait()
        weight = pick[s : s + 1, :1].astype(BF16)
        for stage, held in ((wide_stage, wide_f), (heads_stage, heads_f), (units_stage, units_f)):
            for k in range(held.shape[0]):
                term = stage[s % 2, k] * weight
                held[k] = term if s == 0 else held[k] + term
        if s + 2 < sets:
            for copy in stage_copies(s + 2):
                copy.start()

    def chunk(buffer, c, n, cols=slice(None)):
        rows = buffer[c : c + n, :, :, cols]
        return rows.reshape(n * M, rows.shape[-1])

    def cols_of(g, size):
        return pl.ds(pl.multiple_of(g * size, size), size)

    def project():
        width = math.gcd(H, 256)
        for j in range(3):
            low_j = dot_nt(hidden[...].reshape(S, D), a_q(j)[...]).astype(BF16)
            low_q[j] = low_j

            @pl.loop(0, H // width)
            def _(n, j=j, low_j=low_j):
                cols = cols_of(n, width)
                rows = dot_nn(hidden[...].reshape(S, D), qkv_all[j, :, :, cols].reshape(D, width))
                rows += dot_nn(low_j, b_q(j)[:, cols])
                if j != 1:
                    rows += qkv_bias[pl.ds(j // 2, 1), cols].astype(F32)
                qkv[j, :, cols] = rows.astype(BF16)

    scale = 1.0 / math.sqrt(HEAD)

    def mark_segments():
        row = segments[...].astype(F32)
        pieces = [row[:, q * Q + c * R : q * Q + c * R + R] for c in range(C) for q in range(T)]
        row = jnp.concatenate(pieces, axis=1)
        seg_row[...] = row
        seg_col[...] = jnp.broadcast_to(row, (128, S)).T

    def turn_heads(j):
        @pl.loop(0, heads)
        def _(h):
            turned[cols_of(h, HEAD)] = qkv[j, :, cols_of(h, HEAD)].T

    def attend(c):
        rows = pl.ds(c * M, M)

        @pl.loop(0, heads)
        def _(h):
            cols = cols_of(h, HEAD)
            scores = dot_nt(qkv[1, :, cols], qkv[0, rows, cols]) * scale
            scores = jnp.where(seg_col[:, :1] == seg_row[:, rows], scores, -1e30)
            weights = jnp.exp(scores - jnp.max(scores, axis=0, keepdims=True))
            low = (weights * (1.0 / jnp.sum(weights, axis=0, keepdims=True))).astype(BF16)
            probs[h, :, rows] = low
            mixed[rows, cols] = dot_nn(turned[cols], low).T.astype(BF16)

    def attend_back(c):
        rows = pl.ds(c * M, M)

        @pl.loop(0, heads)
        def _(h):
            cols = cols_of(h, HEAD)
            weights = probs[h, :, rows].astype(F32)
            grad = dot_nt(qkv[2, :, cols], grad_mixed[rows, cols])
            centre = jnp.sum(grad * weights, axis=0, keepdims=True)
            low = (weights * (grad - centre)).astype(BF16)
            grad_scores[:, pl.ds(pl.multiple_of(h * S + c * M, M), M)] = low
            grad_qkv[0, rows, cols] = (dot_nn(turned[cols], low).T * scale).astype(BF16)

    def attend_sums():
        @pl.loop(0, heads)
        def _(h):
            cols = cols_of(h, HEAD)
            low = grad_scores[:, cols_of(h, S)]
            grad_qkv[1, :, cols] = (dot_nn(low, qkv[0, :, cols]) * scale).astype(BF16)
            grad_qkv[2, :, cols] = dot_nn(probs[h], grad_mixed[:, cols]).astype(BF16)

    grad_scores = slope

    def span(c, n):
        return pl.ds(c * M, n * M)

    def put_part(c, n, cols, rows):
        part[c : c + n, :, :, cols] = rows.astype(BF16).reshape(n, T, R, rows.shape[-1])

    group = math.gcd(F, 2)

    def by_blocks(body):
        @pl.loop(0, F // group)
        def _(turn):
            for k in range(group):
                g = turn * group + k
                body(g, cols_of(g, block))

    def mix_out(c, n):
        low = dot_nt(mixed[span(c, n)], a_o[...]).astype(BF16)
        low_o[span(c, n)] = low

        @by_blocks
        def _(g, cols):
            put_part(c, n, cols, dot_nn(mixed[span(c, n)], proj_all[g]) + dot_nn(low, b_o[:, cols]))

    def feed_up(c, n):
        low = dot_nt(chunk(normed, c, n), a_u[...]).astype(BF16)
        low_u[span(c, n)] = low

        @pl.loop(0, FL // NT)
        def _(turn):
            cols = cols_of(turn, NT)
            pre = dot_nn(chunk(normed, c, n), up_all[:, :, cols].reshape(D, NT))
            pre += dot_nn(low, b_u[:, cols]) + up_bias[cols].reshape(1, NT).astype(F32)
            square = pre * pre
            bend = jnp.tanh(ROOT * (pre + 0.044715 * square * pre))
            half = 0.5 * (1.0 + bend)
            act[span(c, n), cols] = (pre * half).astype(BF16)
            rise = half + 0.5 * pre * (1.0 - bend * bend) * (ROOT * (1.0 + 3 * 0.044715 * square))
            slope[span(c, n), cols] = rise.astype(BF16)

    def feed_down(c, n):
        low = dot_nt(act[span(c, n)], a_d[...]).astype(BF16)
        low_d[span(c, n)] = low

        @by_blocks
        def _(g, cols):
            put_part(c, n, cols, dot_nn(act[span(c, n)], down_all[g]) + dot_nn(low, b_d[:, cols]))

    def back_down(c, n):
        low = dot_nt(chunk(grad_feed, c, n), b_d[...]).astype(BF16)
        back_d[span(c, n)] = low

        @pl.loop(0, FL // NT)
        def _(turn):
            cols = cols_of(turn, NT)
            total = dot_nn(low, a_d[:, cols])
            for g in range(F):
                total += dot_nt(chunk(grad_feed, c, n, pl.ds(g * block, block)), down_all[g, cols])
            grad_pre[span(c, n), cols] = (total * slope[span(c, n), cols].astype(F32)).astype(BF16)

    def back_up(c, n):
        low = dot_nt(grad_pre[span(c, n)], b_u[...]).astype(BF16)
        back_u[span(c, n)] = low

        @by_blocks
        def _(g, cols):
            put_part(c, n, cols, dot_nt(grad_pre[span(c, n)], up_all[g]) + dot_nn(low, a_u[:, cols]))

    def back_mix(c, n):
        low = dot_nt(chunk(grad_branch, c, n), b_o[...]).astype(BF16)
        back_o[span(c, n)] = low
        total = dot_nn(low, a_o[...])
        for g in range(F):
            total += dot_nt(chunk(grad_branch, c, n, pl.ds(g * block, block)), proj_all[g])
        grad_mixed[span(c, n)] = total.astype(BF16)

    def back_project(c, n):
        lows = [back_q[j, span(c, n)] for j in range(3)]

        @by_blocks
        def _(g, cols):
            total = dot_nn(lows[0], a_q(0)[:, cols])
            for j in range(3):
                if j:
                    total += dot_nn(lows[j], a_q(j)[:, cols])
                total += dot_nt(grad_qkv[j, span(c, n)], qkv_all[j, g])
            put_part(c, n, cols, total)

    def by_rows(body):
        def all_rows(c):
            rs_end(c)

            @pl.loop(0, R // 16)
            def _(k):
                body(c, cols_of(k, 16), pl.ds(pl.multiple_of(c * R + k * 16, 16), 16))

        return all_rows

    @by_rows
    def meet_one(c, rows, own):
        total = rs_sum(c, rows) + hidden[c, z, rows].astype(F32) + flat(proj_bias)
        unit, rstd = norm_parts(total)
        unit_one[own] = unit
        rstd_one[own] = jnp.broadcast_to(rstd, (16, 128))
        normed[c, z, rows] = (unit * line(gains, 0) + line(shifts, 0)).astype(BF16)

    @by_rows
    def meet_two(c, rows, own):
        total = rs_sum(c, rows) + unit_one[own] * line(gains, 0) + line(shifts, 0) + flat(down_bias)
        unit, rstd = norm_parts(total)
        layer_out[own] = unit * line(gains, 1) + line(shifts, 1)
        grad = norm_pull(cotangent[own].astype(F32) * line(gains, 1), unit, rstd)
        grad_own[own] = grad
        grad_feed[c, z, rows] = grad.astype(BF16)

    @by_rows
    def meet_three(c, rows, own):
        grad = (grad_own[own] + rs_sum(c, rows)) * line(gains, 0)
        grad = norm_pull(grad, unit_one[own], rstd_one[own][:, :1])
        grad_own[own] = grad
        grad_branch[c, z, rows] = grad.astype(BF16)

    @by_rows
    def meet_four(c, rows, own):
        grad_input[own] = grad_own[own] + rs_sum(c, rows)

    def turn_rows(low):
        return low.astype(F32).T.astype(BF16)

    def factor(low, right):
        return dot_nn(turn_rows(low[...]), right).astype(BF16)

    def by_columns(rows, right, place, row):
        count = rows.shape[0]

        @pl.loop(0, T)
        def _(q):
            cols = cols_of(q, H)
            place[pl.ds(row, count), cols] = dot_nn(rows, right[:, :, :, cols].reshape(S, H)).astype(BF16)

    def rows_feed():
        feed_part[pl.ds(0, 16)] = turn_rows(back_u[...])
        feed_part[pl.ds(16, 16)] = turn_rows(low_d[...])

    def units_feed():
        units_g[pl.ds(0, 16)] = factor(low_u, grad_pre[...])
        units_g[pl.ds(16, 16)] = factor(back_d, act[...])

    def wide_feed():
        rows = collect(0)
        by_columns(rows[:16], normed, feed_full, 0)
        by_columns(rows[16:], grad_feed, feed_full, 16)

    def rows_mix():
        for j in range(3):
            low = dot_nt(grad_qkv[j], b_q(j)[...]).astype(BF16)
            back_q[j] = low
            mix_part[pl.ds(16 * j, 16)] = turn_rows(low)
        mix_part[pl.ds(48, 16)] = turn_rows(low_o[...])

    def heads_mix():
        heads_g[pl.ds(48, 16)] = factor(back_o, mixed[...])
        for j in range(3):
            heads_g[pl.ds(16 * j, 16)] = factor(low_q.at[j], grad_qkv[j])
        marks = jnp.concatenate([pick[:, :1], jnp.zeros((32 - sets, 1), F32)])
        heads_g[pl.ds(64, 32)] = jnp.broadcast_to(marks, (32, H)).astype(BF16)

    def wide_mix():
        rows = collect(1)
        by_columns(rows[:48], hidden, mix_full, 0)
        by_columns(rows[48:], grad_branch, mix_full, 48)

    from_low[:, 0] = jnp.zeros((C, R, D), BF16)
    from_high[:, T - 1] = jnp.zeros((C, R, D), BF16)
    qkv_g = gathers[0]
    def own_hidden(step):
        return line_copy(hidden_in, hidden.at[:, z], g_up_send if step > 0 else g_dn_send, g_up_recv if step > 0 else g_dn_recv, C, z, step)

    @pl.when(z < T - 1)
    def _():
        own_hidden(1).start()

    @pl.when(z > 0)
    def _():
        own_hidden(-1).start()

    qkv_g.stage(0)
    for copy in own_copies + stage_copies(0) + stage_copies(1):
        copy.start()
    schedule(cfg, dict(locals()))


def schedule(cfg, env):
    T, C, K = cfg["T"], cfg["C"], env["K"]
    rs, ag, hidden = env["rs"], env["ag"], env["hidden"]
    qkv_g, proj_g, up_g, down_g, rest_g = env["gathers"][:5]
    env["mark_segments"]()
    for s in range(2):
        env["choose"](s)
    for step in range(1, K + 1):
        qkv_g.stage(step)
        if step == 1:
            proj_g.stage(0)
            ag(hidden, None, 2)
            for s in range(2, 5):
                env["choose"](s)
    if K == 0:
        proj_g.stage(0)
    if K >= 1:
        proj_g.stage(1)
    up_g.stage(0)
    if K < 1:
        ag(hidden, None, 2)
        for s in range(2, 5):
            env["choose"](s)
    for s in range(5, env["sets"]):
        env["choose"](s)
    for t in range(3, T + 1):
        ag(hidden, None, t)
    for step in range(2, K + 1):
        proj_g.stage(step)
    down_g.stage(0)
    rest_g.stage(0)
    qkv_g.finish()
    for copy in env["own_copies"]:
        copy.wait()
    env["project"]()
    env["turn_heads"](2)
    if K:
        up_g.stage(1)
    proj_g.finish()
    buffers = [env["normed"], env["grad_feed"], env["grad_branch"]]
    meets = [env["meet_one"], env["meet_two"], env["meet_three"], env["meet_four"]]

    def start_sum(chunks):
        for c in chunks:
            rs(c, 1)

    def work(kind, k, first, n):
        group = range(first, first + n)
        if kind == "up":
            if first == 0:
                up_g.finish()
            env["feed_up"](first, n)
            return
        if kind == "mix":
            env["back_mix"](first, n)
            for c in group:
                env["attend_back"](c)
            return
        if k > 0:
            for c in group:
                env["rs_drain"](c)
        if k == 0:
            for c in group:
                env["attend"](c)
            if first + n == C:
                env["turn_heads"](1)
            env["mix_out"](first, n)
        if k == 1:
            if first == 0:
                for gather in (down_g, rest_g):
                    for step in range(2, K + 1):
                        gather.stage(step)
                down_g.finish()
                rest_g.finish()
            env["feed_down"](first, n)
        if k == 2:
            env["back_down"](first, n)
            env["back_up"](first, n)
        if k == 3:
            env["back_project"](first, n)
        start_sum(group)
        if k == 2 and first + n == C:
            env["rows_feed"]()
            env["deal"](0)
            env["units_feed"]()

    def meet(k, c):
        meets[k](c)
        if k > 0:
            env["ag_drain"](buffers[k - 1], c)
        ag(buffers[k], c, 1)

    steps = []
    for k in range(3):
        steps += [("up", k, 0)] if k == 1 else []
        steps += [("work", k, 0)] + [("rs", k, t) for t in range(2, T)] + [("meet", k, 0)]
        steps += [("ag", k, t) for t in range(2, T + 1)]
    steps.append(("mix", 3, 0))
    groups, at, came, turn = cfg["groups"], [0] * C, {}, 0
    while min(at) < len(steps):
        if turn == 1 and K:
            down_g.stage(1)
            rest_g.stage(1)
        if turn == cfg["up_turn"]:
            for step in range(2, K + 1):
                up_g.stage(step)
        for c in range(C):
            if turn < cfg["lag"] * c or at[c] == len(steps):
                continue
            kind, k, t = steps[at[c]]
            if kind in ("up", "work", "mix"):
                n = groups[k]
                first = c // n * n
                came.setdefault((kind, k, first), set()).add(c)
                if len(came[kind, k, first]) < n:
                    continue
                work(kind, k, first, n)
                for member in range(first, first + n):
                    at[member] += 1
                continue
            if kind == "rs":
                rs(c, t)
            if kind == "meet":
                meet(k, c)
            if kind == "ag":
                ag(buffers[k], c, t)
            at[c] += 1
        turn += 1
    env["attend_sums"]()
    env["rows_mix"]()
    env["deal"](1)
    n, grads = groups[4], env["gathers"][5:]
    for c in range(0, C, n):
        work("work", 3, c, n)

    def shade(piece):
        if piece == 0:
            env["wide_feed"]()
            env["pass_on"](0)
        if piece == 1:
            env["heads_mix"]()
            env["wide_mix"]()
            env["pass_on"](1)
        if piece == 2 and K:
            for gather in grads:
                gather.stage(1)

    hops = [(c, t) for t in range(2, T) for c in range(C)]
    at_hop = [min(len(hops), share) for share in (C // 2, C, C + C // 2)]
    for i in range(len(hops) + 1):
        for piece in range(3):
            if at_hop[piece] == i:
                shade(piece)
        if i < len(hops):
            rs(*hops[i])
    for c in range(C):
        meets[3](c)
        if c == C // 2:
            for step in range(2, K + 1):
                for gather in grads:
                    gather.stage(step)
    for gather in grads:
        gather.finish()
    for c in range(C):
        env["rs_drain"](c)
        env["ag_drain"](buffers[2], c)
    env["ag_drain"](hidden, None)
    for which in range(2):
        env["pass_drain"](which)
    for gather in env["gathers"]:
        gather.drain()


def spread(mesh, body):
    placed = (
        P(("fsdp", "tp"), None),
        P(("fsdp", "tp"), None),
        P("fsdp", None),
        P("fsdp"),
        P(None, "fsdp", "tp"),
        P(None, "tp"),
        P("tp", "fsdp"),
        P(),
        P("fsdp", "tp"),
        P("tp"),
        P("tp", "fsdp"),
        P(),
        P(),
        P(),
        P(),
        P(None, None, None, "tp"),
        P(None, "tp", None),
        P(),
        P(),
        P(None, None, "tp"),
        P(None, "tp", None),
        P(),
    )
    return jax.shard_map(
        body,
        mesh=mesh,
        in_specs=placed,
        out_specs=(
            P(("fsdp", "tp"), None),
            P(("fsdp", "tp"), None),
            P(),
            P(None, None, None, "tp"),
            P(None, "tp", None),
            P(),
            P(),
            P(None, None, "tp"),
            P(None, "tp", None),
            P(),
        ),
        check_vma=False,
    )


def chunks_for(rows):
    return max(c for c in (1, 2, 4) if rows % (16 * c) == 0)


def place_kernel(layer_in, grad_in, feed_in, units_in, mix_in, heads_in, layer_out, grad_out, *refs):
    outs, tables = refs[:8], refs[8:16]
    feed_all, units_all, mix_all, heads_all, rows_a, rows_b, chosen, sems = refs[16:]
    F = feed_all.shape[0]
    sets = outs[2].shape[0]
    loads = [(heads_in, heads_all), (feed_in, feed_all), (units_in, units_all), (mix_in, mix_all)]
    loads += [(layer_in, rows_a), (grad_in, rows_b)]
    loads = [pltpu.make_async_copy(a, b, sems.at[k]) for k, (a, b) in enumerate(loads)]
    stores = list(zip(tables, outs)) + [(rows_a, layer_out), (rows_b, grad_out)]
    stores = [pltpu.make_async_copy(a, b, sems.at[6 + k]) for k, (a, b) in enumerate(stores)]
    for copy in loads:
        copy.start()
    order = lax.broadcasted_iota(jnp.int32, (32, 1), 0).astype(F32)
    q_in, q_out, o_in, o_out, u_in, u_out, d_in, d_out = range(8)
    loads[0].wait()
    for g in range(F):
        marks = heads_all[g, pl.ds(64, 32), pl.ds(0, 128)][:, :1].astype(F32)
        chosen[g] = jnp.clip(jnp.sum(marks * order).astype(jnp.int32), 0, sets - 1)

    def fill(which, rows_of):
        ref = tables[which]
        ref[...] = jnp.zeros_like(ref)

        @pl.loop(0, F)
        def _(g):
            rows_of(ref, g, chosen[g])

        stores[which].start()

    def whole(source, row):
        def add(ref, g, s):
            ref[s] += source[g, pl.ds(row, 16)].astype(F32)

        return add

    def trio(add_of):
        def add(ref, g, s):
            for j in range(3):
                add_of(16 * j)(ref.at[j], g, s)

        return add

    fill(q_out, trio(lambda row: whole(heads_all, row)))
    fill(o_in, whole(heads_all, 48))
    loads[1].wait()
    fill(u_in, whole(feed_all, 0))
    fill(d_out, whole(feed_all, 16))
    loads[2].wait()
    fill(u_out, whole(units_all, 0))
    fill(d_in, whole(units_all, 16))
    loads[3].wait()
    fill(o_out, whole(mix_all, 48))
    fill(q_in, trio(lambda row: whole(mix_all, row)))
    for copy in loads[4:]:
        copy.wait()
    for copy in stores[8:]:
        copy.start()
    for copy in stores:
        copy.wait()


def kernel_per_device(F, T):
    def per_device(
        hidden_in, cotangent, segment_ids, adapter_set, qkv_weight, qkv_bias, proj_weight, proj_bias,
        up_weight, up_bias, down_weight, down_bias, norm_gain, norm_bias, qkv_adapt_in, qkv_adapt_out,
        attn_adapt_in, attn_adapt_out, up_adapt_in, up_adapt_out, down_adapt_in, down_adapt_out,
    ):
        Q, D = hidden_in.shape
        H, FL = qkv_weight.shape[2], up_weight.shape[1]
        S, C, sets = Q * T, chunks_for(Q), qkv_adapt_in.shape[1]
        R, block = Q // C, D // F
        cfg = dict(F=F, T=T, S=S, D=D, H=H, FL=FL, C=C, lag=1, groups=(1, 1, 1, 1, 1), up_turn=T + 1)
        turn = lambda table: jnp.swapaxes(table, -1, -2)
        vmem, anywhere = pl.BlockSpec(memory_space=pltpu.VMEM), pl.BlockSpec(memory_space=pl.ANY)
        dma = pltpu.SemaphoreType.DMA
        bank = lambda *shape: pltpu.VMEM(shape, BF16)
        wide_bank = lambda *shape: pltpu.VMEM(shape, F32)
        scratch = (
            [bank(C, T, R, D), bank(3, F, block, H), bank(F, H, block), bank(F, block, FL), bank(F, FL, block)]
            + [bank(3, S, H), bank(H // HEAD, S, S), bank(S, H), bank(C, T, R, D), bank(S, FL), bank(S, FL)]
            + [bank(C, T, R, D), bank(C, T, R, D), bank(S, H), bank(3, S, H)]
            + [bank(C, T, R, D), bank(C, T, R, D), bank(C, T, R, D)]
            + [wide_bank(Q, D), wide_bank(Q, 128), wide_bank(Q, D)]
            + [bank(3, S, RANK), bank(S, RANK), bank(S, RANK), bank(S, RANK)] * 2
            + [wide_bank(1, S), wide_bank(S, 128), bank(H, S)]
            + [bank(6, RANK, D), bank(4, RANK, H), bank(2, RANK, FL)]
            + [bank(2, 6, RANK, D), bank(2, 4, RANK, H), bank(2, 2, RANK, FL)]
            + [bank(32, S), bank(T - 1, 32, S), bank(32, D)]
            + [bank(64, S), bank(T - 1, 64, S), bank(64, D)]
            + [bank(32, FL), bank(96, H)]
            + [dma((2, 8))] + [dma((2, T - 1))] * 2
            + [dma((9, 2, F)), dma((9, 2, F))]
            + [dma((C, T))] * 4
            + [dma((C + 1, T))] * 4
            + [dma((9,))]
        )
        flops = 2 * S * (4 * D * H + 2 * D * FL) * 2
        outs = pl.pallas_call(
            functools.partial(layer_kernel, cfg),
            out_shape=[
                jax.ShapeDtypeStruct((Q, D), F32),
                jax.ShapeDtypeStruct((Q, D), F32),
                jax.ShapeDtypeStruct((F, 32, D), BF16),
                jax.ShapeDtypeStruct((F, 32, FL), BF16),
                jax.ShapeDtypeStruct((F, 64, D), BF16),
                jax.ShapeDtypeStruct((F, 96, H), BF16),
            ],
            in_specs=[anywhere] + [vmem] * 3 + [anywhere] * 4 + [vmem] * 6 + [anywhere] * 8,
            out_specs=[vmem] * 2 + [anywhere] * 4,
            scratch_shapes=scratch,
            compiler_params=pltpu.CompilerParams(
                collective_id=0, has_side_effects=True, vmem_limit_bytes=62 * 1024 * 1024
            ),
            cost_estimate=pl.CostEstimate(flops=flops, bytes_accessed=30000000, transcendentals=0),
        )(
            hidden_in.reshape(C, R, D), cotangent, segment_ids, adapter_set[None, :],
            qkv_weight, proj_weight, up_weight, down_weight,
            proj_bias, down_bias, up_bias, qkv_bias, norm_gain, norm_bias,
            turn(qkv_adapt_in), qkv_adapt_out, turn(attn_adapt_in), attn_adapt_out,
            turn(up_adapt_in), up_adapt_out, turn(down_adapt_in), down_adapt_out,
        )
        shapes = [
            (3, sets, RANK, D), (3, sets, RANK, H), (sets, RANK, H), (sets, RANK, D),
            (sets, RANK, D), (sets, RANK, FL), (sets, RANK, FL), (sets, RANK, D),
        ]
        table = lambda *shape: jax.ShapeDtypeStruct(shape, F32)
        layer_out, grad_input, q_in, q_out, o_in, o_out, u_in, u_out, d_in, d_out = pl.pallas_call(
            place_kernel,
            out_shape=[table(Q, D), table(Q, D)] + [table(*shape) for shape in shapes],
            in_specs=[anywhere] * 6,
            out_specs=[anywhere] * 10,
            scratch_shapes=[wide_bank(*shape) for shape in shapes]
            + [bank(*out.shape) for out in outs[2:]]
            + [wide_bank(Q, D), wide_bank(Q, D), pltpu.SMEM((F,), jnp.int32), dma((16,))],
            compiler_params=pltpu.CompilerParams(vmem_limit_bytes=62 * 1024 * 1024),
        )(*outs)
        return (
            layer_out, grad_input, turn(q_in), q_out, turn(o_in), o_out, turn(u_in), u_out, turn(d_in), d_out,
        )

    return per_device


def solution(mesh):
    F, T = mesh.shape["fsdp"], mesh.shape["tp"]

    def whole(*args):
        width = args[0].shape[1]
        fits = F & (F - 1) == 0 and (width // F) % 128 == 0 and T > 1 and F > 1 and args[14].shape[1] <= 32 and width // T * args[2].shape[1] <= args[8].shape[1] // T * HEAD
        return spread(mesh, kernel_per_device(F, T) if fits else per_device)(*args)

    return whole
```

profile of v0, /device:TPU:0, one launch (start us, length us, event | category | flops | bytes accessed | tf_op | source)
XLA Modules:
  0.0 296.4 jit_solution(6703742976654135511)
XLA Ops:
  1.3 288.7 %shard_map.285 = (f32[128,2048]{1,0:T(8,128)}, f32[128,2048]{1,0:T(8,128)}, bf16[8,32,2048]{2,1,0:T(8,128)(2,1)}, bf16[8,32,2048]{2,1,0:T(8,128)(2,1)}, bf16[8,6...) custom-call(bf16[4,32,2048]{2,1,0:T(8,128)(2,1)} %bitcast.15, bf16[128,2048]{1,0:T(8,128)(2,1)} %refs_1_.1, ...), custom_call_target="tpu_custom_call" | custom-call | flops 25769803776 | bytes 30000000 | tf_op jit(solution)/shard_map/pallas_call | solution.py:1252
  290.0 6.2 %shard_map.286 = (f32[128,2048]{1,0:T(8,128)}, f32[128,2048]{1,0:T(8,128)}, f32[3,8,16,2048]{3,2,1,0:T(8,128)}, f32[3,8,16,512]{3,2,1,0:T(8,128)}, f32[8,16,512]...) custom-call(f32[128,2048]{1,0:T(8,128)} %get-tuple-element.26.layer_, ...), custom_call_target="tpu_custom_call" | custom-call | tf_op jit(solution)/shard_map/pallas_call | solution.py:1281
where the time goes:
time: 299 us; the launch traced here: 296 us
  Pallas kernels  295 us (99%)
    pallas_call x1, Pallas kernels, per_device(): pl.pallas_call(functools.partial(layer_kernel, cfg), out_shape=[jax.Shape...  289 us
    pallas_call x1, Pallas kernels, per_device(): pl.pallas_call(place_kernel, out_shape=[table(Q, D), table(Q, D)] + [tabl...  6.2 us

commit v1 on v0

--- a/solution.py
+++ b/solution.py
@@ -978,11 +978,9 @@
 
     def work(kind, k, first, n):
         group = range(first, first + n)
-        if kind == "up":
-            if first == 0:
-                up_g.finish()
-            env["feed_up"](first, n)
-            return
+        if kind == "mix" or k in (1, 2):
+            for c in group:
+                ag(buffers[k - 1], c, T)
         if kind == "mix":
             env["back_mix"](first, n)
             for c in group:
@@ -998,6 +996,9 @@
                 env["turn_heads"](1)
             env["mix_out"](first, n)
         if k == 1:
+            if first == 0:
+                up_g.finish()
+            env["feed_up"](first, n)
             if first == 0:
                 for gather in (down_g, rest_g):
                     for step in range(2, K + 1):
@@ -1024,9 +1025,8 @@
 
     steps = []
     for k in range(3):
-        steps += [("up", k, 0)] if k == 1 else []
         steps += [("work", k, 0)] + [("rs", k, t) for t in range(2, T)] + [("meet", k, 0)]
-        steps += [("ag", k, t) for t in range(2, T + 1)]
+        steps += [("ag", k, t) for t in range(2, T)]
     steps.append(("mix", 3, 0))
     groups, at, came, turn = cfg["groups"], [0] * C, {}, 0
     while min(at) < len(steps):
@@ -1040,7 +1040,7 @@
             if turn < cfg["lag"] * c or at[c] == len(steps):
                 continue
             kind, k, t = steps[at[c]]
-            if kind in ("up", "work", "mix"):
+            if kind in ("work", "mix"):
                 n = groups[k]
                 first = c // n * n
                 came.setdefault((kind, k, first), set()).add(c)

time: 299 us -> 291 us (0.973)
  Pallas kernels: 295 us -> 287 us
    pallas_call x1, Pallas kernels: 289 us -> 281 us  [per_device(): pl.pallas_call(functools.partial(layer_kernel, cfg), out_shape=[jax.Shape...]
where the time goes in v1:
time: 291 us; the launch traced here: 289 us
  Pallas kernels  287 us (99%)
    pallas_call x1, Pallas kernels, per_device(): pl.pallas_call(functools.partial(layer_kernel, cfg), out_shape=[jax.Shape...  281 us
    pallas_call x1, Pallas kernels, per_device(): pl.pallas_call(place_kernel, out_shape=[table(Q, D), table(Q, D)] + [tabl...  6.2 us

profile of v1, /device:TPU:0, one launch (start us, length us, event | category | flops | bytes accessed | tf_op | source)
XLA Modules:
  0.0 289.0 jit_solution(106326227494505208)
XLA Ops:
  1.3 281.3 %shard_map.285 = (f32[128,2048]{1,0:T(8,128)}, f32[128,2048]{1,0:T(8,128)}, bf16[8,32,2048]{2,1,0:T(8,128)(2,1)}, bf16[8,32,2048]{2,1,0:T(8,128)(2,1)}, bf16[8,6...) custom-call(bf16[4,32,2048]{2,1,0:T(8,128)(2,1)} %bitcast.15, bf16[128,2048]{1,0:T(8,128)(2,1)} %refs_1_.1, ...), custom_call_target="tpu_custom_call" | custom-call | flops 25769803776 | bytes 30000000 | tf_op jit(solution)/shard_map/pallas_call | solution.py:1252
  282.6 6.2 %shard_map.286 = (f32[128,2048]{1,0:T(8,128)}, f32[128,2048]{1,0:T(8,128)}, f32[3,8,16,2048]{3,2,1,0:T(8,128)}, f32[3,8,16,512]{3,2,1,0:T(8,128)}, f32[8,16,512]...) custom-call(f32[128,2048]{1,0:T(8,128)} %get-tuple-element.26.layer_, ...), custom_call_target="tpu_custom_call" | custom-call | tf_op jit(solution)/shard_map/pallas_call | solution.py:1281

commit v2 on v1

--- a/solution.py
+++ b/solution.py
@@ -1018,6 +1018,8 @@
             env["units_feed"]()
 
     def meet(k, c):
+        if T > 2:
+            rs(c, T - 1)
         meets[k](c)
         if k > 0:
             env["ag_drain"](buffers[k - 1], c)
@@ -1025,7 +1027,7 @@
 
     steps = []
     for k in range(3):
-        steps += [("work", k, 0)] + [("rs", k, t) for t in range(2, T)] + [("meet", k, 0)]
+        steps += [("work", k, 0)] + [("rs", k, t) for t in range(2, T - 1)] + [("meet", k, 0)]
         steps += [("ag", k, t) for t in range(2, T)]
     steps.append(("mix", 3, 0))
     groups, at, came, turn = cfg["groups"], [0] * C, {}, 0

time: 291 us -> 314 us (1.079)
  Pallas kernels: 287 us -> 311 us
    pallas_call x1, Pallas kernels: 281 us -> 305 us  [per_device(): pl.pallas_call(functools.partial(layer_kernel, cfg), out_shape=[jax.Shape...]
where the time goes in v2:
time: 314 us; the launch traced here: 312 us
  Pallas kernels  311 us (99%)
    pallas_call x1, Pallas kernels, per_device(): pl.pallas_call(functools.partial(layer_kernel, cfg), out_shape=[jax.Shape...  305 us

profile of v2, /device:TPU:0, one launch (start us, length us, event | category | flops | bytes accessed | tf_op | source)
XLA Modules:
  0.0 312.2 jit_solution(3135599372557855307)
XLA Ops:
  1.3 304.5 %shard_map.285 = (f32[128,2048]{1,0:T(8,128)}, f32[128,2048]{1,0:T(8,128)}, bf16[8,32,2048]{2,1,0:T(8,128)(2,1)}, bf16[8,32,2048]{2,1,0:T(8,128)(2,1)}, bf16[8,6...) custom-call(bf16[4,32,2048]{2,1,0:T(8,128)(2,1)} %bitcast.15, bf16[128,2048]{1,0:T(8,128)(2,1)} %refs_1_.1, ...), custom_call_target="tpu_custom_call" | custom-call | flops 25769803776 | bytes 30000000 | tf_op jit(solution)/shard_map/pallas_call | solution.py:1254
  305.8 6.2 %shard_map.286 = (f32[128,2048]{1,0:T(8,128)}, f32[128,2048]{1,0:T(8,128)}, f32[3,8,16,2048]{3,2,1,0:T(8,128)}, f32[3,8,16,512]{3,2,1,0:T(8,128)}, f32[8,16,512]...) custom-call(f32[128,2048]{1,0:T(8,128)} %get-tuple-element.26.layer_, ...), custom_call_target="tpu_custom_call" | custom-call | tf_op jit(solution)/shard_map/pallas_call | solution.py:1283
